TPU v7x, 512 devices: a whole 4x4x16 slice. The times are simulated.
512 devices in a mesh: dp: 16 (over x, y_hi, core), space: 32 (over y_lo, z).
Axes of the slice: x: 4, y: 4 (y_hi: 2, y_lo: 2; y = y_hi * 2 + y_lo), z: 16, core: 2. Of those that a mesh axis runs over, the one named last changes fastest.
Arguments:
- queries: bfloat16 [16, 1120, 8192], P('dp', None, 'space'), may hold values from -6 to 6
- keys: bfloat16 [16, 1120, 8192], P('dp', None, 'space'), may hold values from -6 to 6
- values: bfloat16 [16, 1120, 8192], P('dp', None, 'space'), may hold values from -5.5 to 5.5
- out_grad: bfloat16 [16, 1120, 8192], P('dp', None, 'space'), may hold values from -6 to 6
- q_gain: float32 [1120], replicated, may hold values from 0.5 to 1.5
- k_gain: float32 [1120], replicated, may hold values from 0.5 to 1.5
Outputs:
- grad_queries: bfloat16 [16, 1120, 8192], P('dp', None, 'space')
- grad_keys: bfloat16 [16, 1120, 8192], P('dp', None, 'space')
- grad_values: bfloat16 [16, 1120, 8192], P('dp', None, 'space')
- grad_q_gain: float32 [1120], replicated
- grad_k_gain: float32 [1120], replicated
All inputs are finite; a program needn't handle non-finite values.
Results may differ from a plain program's by a relative error of at most 0.0055.
Values sent between devices are 32-bit elements; how exact they have to be, the bound alone decides.
A program may use at most 64 MiB of HBM per device.

v0:
```python
import math

import jax
import jax.numpy as jnp
from jax import lax
from jax.sharding import PartitionSpec as P

HEADS = 10
HEAD_DIM = 112


norm_eps = 1e-06
denom_eps = 1e-06
highest = lax.Precision.HIGHEST


def normalize(inputs, gain):
    floats = inputs.astype(jnp.float32).reshape(HEADS, HEAD_DIM, -1)
    inverse = lax.rsqrt(jnp.mean(floats * floats, axis=1, keepdims=True) + norm_eps)
    unit = floats * inverse
    return (unit, inverse, unit * gain.reshape(HEADS, HEAD_DIM, 1))


def features(normed):
    rounded = jnp.maximum(normed, 0.0).astype(jnp.bfloat16)
    rounded = lax.optimization_barrier(rounded)
    return (rounded, rounded.astype(jnp.float32))


def norm_backward(grad_normed, unit, inverse, gain):
    upstream = grad_normed * gain.reshape(HEADS, HEAD_DIM, 1)
    grad_in = inverse * (upstream - unit * jnp.mean(upstream * unit, axis=1, keepdims=True))
    return (
        grad_in.reshape(HEADS * HEAD_DIM, -1).astype(jnp.bfloat16),
        jnp.sum(grad_normed * unit, axis=2),
    )


def local(queries, keys, values, out_grad, q_gain, k_gain):
    tokens_here = queries.shape[2]
    clip_tokens = tokens_here * lax.axis_size("space")
    all_rows = clip_tokens * queries.shape[0] * lax.axis_size("dp")
    loss_scale = math.sqrt(clip_tokens)
    unit_query, inverse_query, normed_query = normalize(queries[0], q_gain)
    unit_key, inverse_key, normed_key = normalize(keys[0], k_gain)
    feature_qb, feature_query = features(normed_query)
    feature_kb, feature_key = features(normed_key)
    value_heads = values[0].reshape(HEADS, HEAD_DIM, tokens_here)
    grad_heads = out_grad[0].astype(jnp.float32).reshape(HEADS, HEAD_DIM, tokens_here)
    state_part = jnp.einsum(
        "hct,hdt->hcd", feature_kb, value_heads, preferred_element_type=jnp.float32
    )
    key_part = jnp.sum(feature_key, axis=2)
    state, key_total = lax.psum((state_part, key_part), "space")
    denominator = jnp.einsum("hct,hc->ht", feature_query, key_total, precision=highest) + denom_eps
    attended = (
        jnp.einsum("hct,hcd->hdt", feature_query, state, precision=highest)
        / denominator[:, None, :]
    )
    scaled = loss_scale * grad_heads / denominator[:, None, :]
    projected = jnp.sum(attended * scaled, axis=1)
    grad_state_part = jnp.einsum("hct,hdt->hcd", feature_query, scaled, precision=highest)
    grad_key_part = -jnp.einsum("hct,ht->hc", feature_query, projected, precision=highest)
    grad_state, grad_key_total = lax.psum((grad_state_part, grad_key_part), "space")
    grad_feat_q = (
        jnp.einsum("hcd,hdt->hct", state, scaled, precision=highest)
        - key_total[:, :, None] * projected[:, None, :]
    )
    grad_normed_q = jnp.where(normed_query > 0, grad_feat_q, 0.0)
    grad_query, part_query = norm_backward(grad_normed_q, unit_query, inverse_query, q_gain)
    value_float = value_heads.astype(jnp.float32)
    grad_feat_k = (
        jnp.einsum("hcd,hdt->hct", grad_state, value_float, precision=highest)
        + grad_key_total[:, :, None]
    )
    grad_value = jnp.einsum("hcd,hct->hdt", grad_state, feature_key, precision=highest)
    grad_value = grad_value.reshape(HEADS * HEAD_DIM, tokens_here).astype(jnp.bfloat16)
    grad_normed_k = jnp.where(normed_key > 0, grad_feat_k, 0.0)
    grad_key, part_key = norm_backward(grad_normed_k, unit_key, inverse_key, k_gain)
    total_query, total_key = lax.psum((part_query, part_key), ("dp", "space"))
    divisor = math.sqrt(all_rows)
    grad_q_gain = (total_query / divisor).reshape(HEADS * HEAD_DIM)
    grad_k_gain = (total_key / divisor).reshape(HEADS * HEAD_DIM)
    return (grad_query[None], grad_key[None], grad_value[None], grad_q_gain, grad_k_gain)


def solution(mesh):
    in_specs = (
        P("dp", None, "space"),
        P("dp", None, "space"),
        P("dp", None, "space"),
        P("dp", None, "space"),
        P(),
        P(),
    )
    out_specs = (P("dp", None, "space"), P("dp", None, "space"), P("dp", None, "space"), P(), P())
    return jax.shard_map(local, mesh=mesh, in_specs=in_specs, out_specs=out_specs, check_vma=False)
```

profile of v0, /device:TPU:1, one launch (start us, length us, event | category | flops | bytes accessed | tf_op | source)
XLA Modules:
  0.0 520.5 jit_solution(6007839253031318226)
XLA Ops:
  7.2 0.9 mul.130
  8.1 0.8 mul.136
  8.9 1.2 fusion.23
  10.1 1.2 fusion.29
  11.6 0.2 convert_reduce_fusion
  11.8 58.3 %psum.43 = f32[10,112]{1,0:T(8,128)S(1)} all-reduce(f32[10,112]{1,0:T(8,128)S(1)} %convert_reduce_fusion), channel_id=1, replica_groups=mesh['dp'=16,'space'=32] {'space'}, use_global_device_ids=true, to_apply=%region_4.0 | all-reduce | flops 1120 | bytes 8960 | tf_op jit(solution)/shard_map/psum | solution.py:54
  70.1 1.1 fusion.35
  71.5 0.3 fusion.32
  71.8 0.5 copy-done.7
  72.4 1.0 copy-done.4
  73.4 1.6 fusion.34
  75.0 242.3 %all-reduce.4.cloned.1.call-done = (f32[10,112,112]{2,1,0:T(8,128)}, f32[10,112,112]{2,1,0:T(8,128)}) async-done(((f32[10,112,112]{2,1,0:T(8,128)}, f32[10,112,112]{2,1,0:T(8,128)}), (f32[10,112,112]{2,1,0:T(8,128)}, f32[10,112,112]{2,1,0:T(8,128)})) %all-reduce.4.cloned.1.call-update) | async-done | bytes 1003536 | tf_op jit(solution)/shard_map/psum | solution.py:54
  317.3 2.7 convolution_convert_fusion
  319.9 0.8 fusion.15
  320.7 2.6 fusion.22
  323.3 0.5 fusion.30
  323.8 48.2 %psum.45 = f32[10,112]{1,0:T(8,128)S(1)} all-reduce(f32[10,112]{1,0:T(8,128)S(1)} %bitcast_negate_fusion), channel_id=1, replica_groups=mesh['dp'=16,'space'=32] {'space'}, use_global_device_ids=true, to_apply=%region_8.9 | all-reduce | flops 1120 | bytes 8960 | tf_op jit(solution)/shard_map/psum | solution.py:64
  372.0 2.0 fusion.28
  374.1 135.8 %all-reduce = (f32[10,112]{1,0:T(8,128)S(1)}, f32[10,112]{1,0:T(8,128)S(1)}) all-reduce(f32[10,112]{1,0:T(8,128)S(1)} %get-tuple-element.7, f32[10,112]{1,0:T(8,128)S(1)} %get-tuple-element.5), channel_id=1, replica_groups=mesh['dp'=16,'space'=32] {'dp','space'}, use_global_device_ids=true, to_apply=%region_11.12 | all-reduce | flops 2240 | bytes 17920 | tf_op jit(solution)/shard_map/psum | solution.py:80
  509.9 0.7 reshape.100
  510.6 0.7 reshape.99
  511.2 1.1 fusion.21
  512.3 0.3 copy-done.6
  512.6 1.1 fusion.27
  (29 shorter events, 0.7 us)
Async XLA Ops:
  7.2 62.9 %copy-start = (bf16[1,1120,256]{2,1,0:T(8,128)(2,1)S(1)}, bf16[1,1120,256]{2,1,0:T(8,128)(2,1)}, u32[]{:S(2)}) copy-start(bf16[1,1120,256]{2,1,0:T(8,128)(2,1)} %param.8) | copy-start | bytes 1720324
  7.2 4.1 copy-start.2
  7.2 310.1 %all-reduce.4.cloned.1.call-start = ((), (), s32[]{:S(2)}) async-start(), calls=%async_computation | async-start | bytes 2293760 | tf_op jit(solution)/shard_map/psum | solution.py:54
  11.6 59.7 %copy-start.1 = (bf16[1,1120,256]{2,1,0:T(8,128)(2,1)S(1)}, bf16[1,1120,256]{2,1,0:T(8,128)(2,1)}, u32[]{:S(2)}) copy-start(bf16[1,1120,256]{2,1,0:T(8,128)(2,1)} %param.6) | copy-start | bytes 1720324
  71.2 1.1 copy-start.7
  72.4 1.0 copy-start.4
  317.3 2.7 copy-start.5
  317.3 2.7 copy-start.9
  320.7 51.3 %copy-start.8 = (f32[10,112,112]{2,1,0:T(8,128)S(1)}, f32[10,112,112]{2,1,0:T(8,128)}, u32[]{:S(2)}) copy-start(f32[10,112,112]{2,1,0:T(8,128)} %get-tuple-element.12) | copy-start | bytes 1505284
  372.0 139.2 %copy-start.3 = (f32[10,112,256]{2,1,0:T(8,128)S(1)}, f32[10,112,256]{2,1,0:T(8,128)}, u32[]{:S(2)}) copy-start(f32[10,112,256]{2,1,0:T(8,128)} %get-tuple-element.13) | copy-start | bytes 3440644
  511.2 1.4 copy-start.6
Sparse Core Ops, SparseCore 0:
  75.1 242.0 all-reduce.3
where the time goes:
time: 521 us
  blocking collectives  242 us (46%)
  waiting for transfers between devices  242 us (46%)
  between operations  14.2 us (3%)
  matrix products  11.6 us (2%)
  other arithmetic  5.44 us (1%)
    psum x1, waiting for transfers between devices, local(): state, key_total = lax.psum((state_part, key_part), 'space')  242 us
    psum x1, blocking collectives, local(): total_query, total_key = lax.psum((part_query, part_key), ('dp', 'space'))  136 us
    psum x1, blocking collectives, local(): state, key_total = lax.psum((state_part, key_part), 'space')  58.3 us
    psum x1, blocking collectives, local(): lax.psum((grad_state_part, grad_key_part), 'space')  48.2 us
  transfers between devices with their start and end apart: 1, of which 1 were waited for; matrix products, arithmetic and copies ran while one was open for 0% of the time, Pallas kernels for 0%

commit v1 on v0

v1 whole, which is shorter than its diff:
```python
import math

import jax
import jax.numpy as jnp
from jax import lax
from jax.experimental import pallas as pl
from jax.experimental.pallas import tpu as pltpu
from jax.sharding import PartitionSpec as P

HEADS = 10
HEAD_DIM = 112
CH = HEADS * HEAD_DIM
LANES = 128
SPLIT_HEAD = 7
SPARE = LANES - HEAD_DIM
HOSTS = HEAD_DIM // SPARE
ROWS = 1024
PIECES = 4
PIECE = ROWS // PIECES
HALF = PIECE // 2
QUARTER = HALF // 4
OWN = QUARTER // 4
Y, Z = 2, 16

norm_eps = 1e-06
denom_eps = 1e-06
F32 = jnp.float32
BF16 = jnp.bfloat16
MESH = pl.DeviceIdType.MESH
NT = (((1,), (1,)), ((), ()))
NN = (((1,), (0,)), ((), ()))
TN = (((0,), (0,)), ((), ()))


def dot(a, b, dims):
    return lax.dot_general(a, b, dims, preferred_element_type=F32)


def split(x):
    high = x.astype(BF16)
    return high, (x - high.astype(F32)).astype(BF16)


def rows_of(head):
    return pl.ds(head * HEAD_DIM, HEAD_DIM)


def block_of(head):
    return pl.ds((head if head < SPLIT_HEAD else head - 1) * HEAD_DIM, HEAD_DIM)


def kernel(
    clip_tokens,
    all_rows,
    dps,
    q_hbm,
    k_hbm,
    v_hbm,
    g_hbm,
    gains_ref,
    gq_hbm,
    gk_hbm,
    gv_hbm,
    gain_out,
    q_in,
    k_in,
    v_in,
    g_in,
    feat_q,
    feat_k,
    inv_q,
    inv_k,
    rden,
    scaled_hi,
    scaled_lo,
    grad_f,
    out_q,
    out_k,
    out_v,
    gain_col,
    kt_col,
    part,
    recv_y,
    half,
    recv_w,
    quarter,
    recv_s,
    full,
    one_a,
    one_b,
    two_a,
    two_b,
    three,
    load_sem,
    store_sem,
    big_send,
    big_recv,
    small_send,
    small_recv,
):
    tokens = q_in.shape[1]
    dp = lax.axis_index("dp")
    space = lax.axis_index("space")
    y, z = space // Z, space % Z
    k4, g4 = z % 4, z // 4
    sign = 1 - 2 * (dp % 2)

    def at(dy, dz):
        return (dp, lax.rem(y + dy, Y) * Z + lax.rem(z + dz + 2 * Z, Z))

    loads = [
        pltpu.make_async_copy(src.at[0], dst, load_sem.at[i])
        for i, (src, dst) in enumerate(
            ((k_hbm, k_in), (v_hbm, v_in), (q_hbm, q_in), (g_hbm, g_in))
        )
    ]
    for load in loads:
        load.start()

    barrier = pltpu.get_barrier_semaphore()

    def cluster_peer(r):
        return (dp, lax.rem(y + r // 4, Y) * Z + g4 * 4 + lax.rem(k4 + r % 4, 4))

    greeted = 0
    for r in range(1, 8):
        pl.semaphore_signal(barrier, inc=1, device_id=cluster_peer(r), device_id_type=MESH)
        greeted += 1
    for dz in (1, -1, 2, -2, 4, -4, 8):
        pl.semaphore_signal(barrier, inc=1, device_id=at(0, dz), device_id_type=MESH)
        greeted += 1
    for r in range(1, dps):
        pl.semaphore_signal(
            barrier, inc=1, device_id=(lax.rem(dp + r, dps), space), device_id_type=MESH
        )
        greeted += 1

    lane = lax.broadcasted_iota(jnp.int32, (HEAD_DIM, LANES), 1)
    ones = jnp.ones((16, tokens), BF16)
    no_rows = jnp.zeros((SPARE, tokens), BF16)

    gain_col[...] = jnp.transpose(gains_ref[...])

    def q_gain(h):
        return gain_col[0:HEAD_DIM, h : h + 1]

    def k_gain(h):
        return gain_col[0:HEAD_DIM, 16 + h : 17 + h]

    def pad(x):
        return jnp.concatenate([x, no_rows], axis=0)

    def features(x_in, inv_ref, gain, feat_ref, h):
        x = x_in[rows_of(h), :].astype(F32)
        inverse = lax.rsqrt(jnp.sum(x * x, axis=0, keepdims=True) * (1.0 / HEAD_DIM) + norm_eps)
        inv_ref[h : h + 1, :] = inverse
        feat = jnp.maximum((x * inverse) * gain(h), 0.0).astype(BF16)
        feat_ref[rows_of(h), :] = feat
        return feat

    def place(a, h, block, spread):
        if h < HOSTS:
            moved = pltpu.roll(spread, (HEAD_DIM - SPARE * h) % LANES, 1)
            block = jnp.where(lane >= HEAD_DIM, moved, block)
        part[a, block_of(h), :] = block

    def take(a, h):
        if h != SPLIT_HEAD:
            return full[a, block_of(h), :][:, 0:HEAD_DIM]
        whole = jnp.zeros((HEAD_DIM, LANES), F32)
        for j in range(HOSTS):
            moved = pltpu.roll(full[a, block_of(j), :], (SPARE * j - HEAD_DIM) % LANES, 1)
            whole = jnp.where((lane >= SPARE * j) & (lane < SPARE * (j + 1)), moved, whole)
        return whole[:, 0:HEAD_DIM]

    order = [SPLIT_HEAD] + [h for h in range(HEADS) if h != SPLIT_HEAD]
    tail = pl.ds((HEADS - 1) * HEAD_DIM, ROWS - (HEADS - 1) * HEAD_DIM)

    def big(a, p, slot, src, dst, peer):
        return pltpu.make_async_remote_copy(
            src_ref=src,
            dst_ref=dst,
            send_sem=big_send.at[a, p, slot],
            recv_sem=big_recv.at[a, p, slot],
            device_id=peer,
            device_id_type=MESH,
        )

    sent = []

    def go(copies):
        for copy in copies:
            copy.start()
            sent.append(copy)
        return copies

    def land(copies):
        for copy in copies:
            copy.wait_recv()

    window = (sign, -sign, -2 * sign)
    stride = (4, 12, 8)

    def rs_y(a, p):
        other = lax.rem(y + 1, Y)
        src = part.at[a, pl.ds(pl.multiple_of(p * PIECE + other * HALF, HALF), HALF)]
        return go([big(a, p, 0, src, recv_y.at[a, p], at(1, 0))])

    def rs_w(a, p, came):
        land(came)
        mine = pl.ds(pl.multiple_of(p * PIECE + y * HALF, HALF), HALF)
        half[a, p] = part[a, mine, :] + recv_y[a, p]
        copies = []
        for m, dz in enumerate(window):
            kind = lax.rem(z + dz + Z, 4)
            src = half.at[a, p, pl.ds(pl.multiple_of(kind * QUARTER, QUARTER), QUARTER)]
            copies.append(big(a, p, 1 + m, src, recv_w.at[a, p, m], at(0, dz)))
        return go(copies)

    def rs_s(a, p, came):
        land(came)
        mine = pl.ds(pl.multiple_of(k4 * QUARTER, QUARTER), QUARTER)
        quarter[a, p] = (half[a, p, mine, :] + recv_w[a, p, 0]) + (
            recv_w[a, p, 1] + recv_w[a, p, 2]
        )
        copies = []
        for m, dz in enumerate(stride):
            group = lax.rem(g4 + dz // 4, 4)
            src = quarter.at[a, p, pl.ds(pl.multiple_of(group * OWN, OWN), OWN)]
            copies.append(big(a, p, 4 + m, src, recv_s.at[a, p, m], at(0, dz)))
        return go(copies)

    def ag_s(a, p, came):
        land(came)
        own = pl.ds(pl.multiple_of(g4 * OWN, OWN), OWN)
        place_own = pl.ds(
            pl.multiple_of(p * PIECE + y * HALF + k4 * QUARTER + g4 * OWN, OWN), OWN
        )
        full[a, place_own, :] = (quarter[a, p, own, :] + recv_s[a, p, 0]) + (
            recv_s[a, p, 1] + recv_s[a, p, 2]
        )
        ref = full.at[a, place_own]
        return go([big(a, p, 7 + m, ref, ref, at(0, dz)) for m, dz in enumerate(stride)])

    def ag_w(a, p, came):
        land(came)
        ref = full.at[
            a, pl.ds(pl.multiple_of(p * PIECE + y * HALF + k4 * QUARTER, QUARTER), QUARTER)
        ]
        return go([big(a, p, 10 + m, ref, ref, at(0, dz)) for m, dz in enumerate(window)])

    def ag_y(a, p, came):
        land(came)
        ref = full.at[a, pl.ds(pl.multiple_of(p * PIECE + y * HALF, HALF), HALF)]
        return go([big(a, p, 13, ref, ref, at(1, 0))])

    def small(slot, ref, peer):
        return pltpu.make_async_remote_copy(
            src_ref=ref,
            dst_ref=ref,
            send_sem=small_send.at[slot],
            recv_sem=small_recv.at[slot],
            device_id=peer,
            device_id_type=MESH,
        )

    def small_cluster(base, buf):
        ref = buf.at[y * 4 + k4]
        return go([small(base + r, ref, cluster_peer(r)) for r in range(1, 8)])

    def small_stride(base, came, buf_a, buf_b):
        land(came)
        total = buf_a[0]
        for e in range(1, 8):
            total = total + buf_a[e]
        buf_b[g4] = total
        ref = buf_b.at[g4]
        return go([small(base + m, ref, at(0, dz)) for m, dz in enumerate(stride)])

    def small_done(came, buf_b):
        land(came)
        return (buf_b[0] + buf_b[1]) + (buf_b[2] + buf_b[3])

    cell = y * 4 + k4
    one_a[cell] = jnp.zeros_like(one_a[cell])
    two_a[cell] = jnp.zeros_like(two_a[cell])
    part[0, tail, :] = jnp.zeros((tail.size, LANES), F32)
    part[1, tail, :] = jnp.zeros((tail.size, LANES), F32)

    loads[0].wait()
    loads[1].wait()
    spread = None
    for h in order:
        feat = features(k_in, inv_k, k_gain, feat_k, h)
        one_a[cell, h : h + 1, 0:HEAD_DIM] = dot(ones, feat, NT)[0:1]
        block = dot(feat, pad(v_in[rows_of(h), :]), NT)
        if h == SPLIT_HEAD:
            spread = block
        else:
            place(0, h, block, spread)
    loads[2].wait()
    for h in order:
        features(q_in, inv_q, q_gain, feat_q, h)
    loads[3].wait()

    pl.semaphore_wait(barrier, greeted)
    pieces = range(PIECES)
    ar1 = small_cluster(0, one_a)
    s = [rs_y(0, p) for p in pieces]
    ar1 = small_stride(8, ar1, one_a, one_b)
    s = [rs_w(0, p, s[p]) for p in pieces]
    s = [rs_s(0, p, s[p]) for p in pieces]

    key_total = small_done(ar1, one_b)
    kt_col[...] = jnp.transpose(key_total)
    kt_hi, kt_rest = split(key_total)
    kt_mid = kt_rest
    kt_lo = (key_total - kt_hi.astype(F32) - kt_mid.astype(F32)).astype(BF16)
    kt3 = jnp.concatenate([kt_hi, kt_mid, kt_lo], axis=0)[:, 0:HEAD_DIM]
    loss_scale = math.sqrt(clip_tokens)
    for h in order:
        feat = feat_q[rows_of(h), :]
        terms = dot(kt3, feat, NN)
        denominator = (
            terms[h : h + 1] + (terms[16 + h : 17 + h] + terms[32 + h : 33 + h])
        ) + denom_eps
        inverse = 1.0 / denominator
        rden[h : h + 1, :] = inverse
        scaled = g_in[rows_of(h), :].astype(F32) * (loss_scale * inverse)
        high, low = split(scaled)
        scaled_hi[rows_of(h), :] = high
        scaled_lo[rows_of(h), :] = low
        block = dot(feat, pad(high), NT) + dot(feat, pad(low), NT)
        if h == SPLIT_HEAD:
            spread = block
        else:
            place(1, h, block, spread)

    g = [rs_y(1, p) for p in pieces]
    s = [ag_s(0, p, s[p]) for p in pieces]
    g = [rs_w(1, p, g[p]) for p in pieces]
    s = [ag_w(0, p, s[p]) for p in pieces]
    g = [rs_s(1, p, g[p]) for p in pieces]
    s = [ag_y(0, p, s[p]) for p in pieces]
    for p in pieces:
        land(s[p])

    for h in range(HEADS):
        feat = feat_q[rows_of(h), :]
        high, low = scaled_hi[rows_of(h), :], scaled_lo[rows_of(h), :]
        state_hi, state_lo = split(take(0, h))
        grad = dot(state_hi, high, NN) + (dot(state_lo, high, NN) + dot(state_hi, low, NN))
        feat_f = feat.astype(F32)
        projected = jnp.sum(feat_f * grad, axis=0, keepdims=True) * rden[h : h + 1, :]
        grad = grad - kt_col[0:HEAD_DIM, h : h + 1] * projected
        grad_f[rows_of(h), :] = grad
        p_hi, p_lo = split(-projected)
        two_a[cell, h : h + 1, 0:HEAD_DIM] = (
            dot(jnp.broadcast_to(p_hi, (16, tokens)), feat, NT)
            + dot(jnp.broadcast_to(p_lo, (16, tokens)), feat, NT)
        )[0:1]
        e_hi, e_lo = split(feat_f * grad)
        two_a[cell, HEADS + h : HEADS + h + 1, 0:HEAD_DIM] = (
            dot(ones, e_hi, NT) + dot(ones, e_lo, NT)
        )[0:1]
    ar2 = small_cluster(16, two_a)

    g = [ag_s(1, p, g[p]) for p in pieces]

    def norm_backward(x_in, inv_ref, gain, feat, grad, out, h):
        inverse = inv_ref[h : h + 1, :]
        unit = x_in[rows_of(h), :].astype(F32) * inverse
        upstream = jnp.where(feat > 0, grad, 0.0) * gain(h)
        mean = jnp.sum(upstream * unit, axis=0, keepdims=True) * (1.0 / HEAD_DIM)
        out[rows_of(h), :] = (inverse * (upstream - unit * mean)).astype(BF16)

    def grad_queries(heads):
        for h in heads:
            feat = feat_q[rows_of(h), :].astype(F32)
            norm_backward(q_in, inv_q, q_gain, feat, grad_f[rows_of(h), :], out_q, h)

    grad_queries(range(HEADS))
    store_q = pltpu.make_async_copy(out_q, gq_hbm.at[0], store_sem.at[0])
    store_q.start()
    ar2 = small_stride(24, ar2, two_a, two_b)
    g = [ag_w(1, p, g[p]) for p in pieces]
    g = [ag_y(1, p, g[p]) for p in pieces]
    for p in pieces:
        land(g[p])

    for h in range(HEADS):
        gs_hi, gs_lo = split(take(1, h))
        value = v_in[rows_of(h), :]
        feat = feat_k[rows_of(h), :]
        out_v[rows_of(h), :] = (dot(gs_hi, feat, TN) + dot(gs_lo, feat, TN)).astype(BF16)
        grad_f[rows_of(h), :] = dot(gs_hi, value, NN) + dot(gs_lo, value, NN)
    store_v = pltpu.make_async_copy(out_v, gv_hbm.at[0], store_sem.at[1])
    store_v.start()

    total = small_done(ar2, two_b)
    three[dp] = total
    ref = three.at[dp]
    ar3 = go([small(32 + r, ref, (lax.rem(dp + r, dps), space)) for r in range(1, dps)])
    gkt_col = jnp.transpose(total)
    for h in range(HEADS):
        feat = feat_k[rows_of(h), :].astype(F32)
        grad = grad_f[rows_of(h), :] + gkt_col[0:HEAD_DIM, h : h + 1]
        norm_backward(k_in, inv_k, k_gain, feat, grad, out_k, h)
    store_k = pltpu.make_async_copy(out_k, gk_hbm.at[0], store_sem.at[2])
    store_k.start()

    land(ar3)
    total = three[0]
    for r in range(1, dps):
        total = total + three[r]
    gain_sum = total[HEADS : 2 * HEADS, 0:HEAD_DIM] * (1.0 / math.sqrt(all_rows))
    gain_out[0] = gain_sum / gains_ref[0:HEADS, 0:HEAD_DIM]
    gain_out[1] = gain_sum / gains_ref[16 : 16 + HEADS, 0:HEAD_DIM]

    for copy in sent:
        copy.wait_send()
    store_q.wait()
    store_v.wait()
    store_k.wait()


def local(queries, keys, values, out_grad, q_gain, k_gain):
    tokens = queries.shape[2]
    dps = lax.axis_size("dp")
    clip_tokens = tokens * lax.axis_size("space")
    all_rows = clip_tokens * dps * queries.shape[0]
    gains = jnp.concatenate(
        [
            jnp.pad(g.reshape(HEADS, HEAD_DIM), ((0, 16 - HEADS), (0, SPARE)), constant_values=1.0)
            for g in (q_gain, k_gain)
        ]
    )
    anywhere = pl.BlockSpec(memory_space=pl.ANY)
    here = pl.BlockSpec(memory_space=pltpu.VMEM)
    big = jax.ShapeDtypeStruct(queries.shape, BF16)
    vm = pltpu.VMEM
    dma = pltpu.SemaphoreType.DMA

    def run(*refs):
        kernel(clip_tokens, all_rows, dps, *refs)

    grad_q, grad_k, grad_v, gain_grads = pl.pallas_call(
        run,
        out_shape=(big, big, big, jax.ShapeDtypeStruct((2, HEADS, HEAD_DIM), F32)),
        in_specs=[anywhere] * 4 + [here],
        out_specs=(anywhere, anywhere, anywhere, here),
        scratch_shapes=[
            vm((CH, tokens), BF16),
            vm((CH, tokens), BF16),
            vm((CH, tokens), BF16),
            vm((CH, tokens), BF16),
            vm((CH, tokens), BF16),
            vm((CH, tokens), BF16),
            vm((16, tokens), F32),
            vm((16, tokens), F32),
            vm((16, tokens), F32),
            vm((CH, tokens), BF16),
            vm((CH, tokens), BF16),
            vm((CH, tokens), F32),
            vm((CH, tokens), BF16),
            vm((CH, tokens), BF16),
            vm((CH, tokens), BF16),
            vm((LANES, 32), F32),
            vm((LANES, 16), F32),
            vm((2, ROWS, LANES), F32),
            vm((2, PIECES, HALF, LANES), F32),
            vm((2, PIECES, HALF, LANES), F32),
            vm((2, PIECES, 3, QUARTER, LANES), F32),
            vm((2, PIECES, QUARTER, LANES), F32),
            vm((2, PIECES, 3, OWN, LANES), F32),
            vm((2, ROWS, LANES), F32),
            vm((8, 16, LANES), F32),
            vm((4, 16, LANES), F32),
            vm((8, 24, LANES), F32),
            vm((4, 24, LANES), F32),
            vm((dps, 24, LANES), F32),
            dma((4,)),
            dma((3,)),
            dma((2, PIECES, 14)),
            dma((2, PIECES, 14)),
            dma((32 + 16,)),
            dma((32 + 16,)),
        ],
        compiler_params=pltpu.CompilerParams(
            collective_id=0, has_side_effects=True, vmem_limit_bytes=48 << 20
        ),
        name="linear_attention_backward",
    )(queries, keys, values, out_grad, gains)
    return (
        grad_q,
        grad_k,
        grad_v,
        gain_grads[0].reshape(CH),
        gain_grads[1].reshape(CH),
    )


def solution(mesh):
    whole = P("dp", None, "space")
    return jax.shard_map(
        local,
        mesh=mesh,
        in_specs=(whole, whole, whole, whole, P(), P()),
        out_specs=(whole, whole, whole, P(), P()),
        check_vma=False,
    )
```

time: 521 us -> 91.7 us (0.18)
  blocking collectives: 242 us -> 0 us
  waiting for transfers between devices: 242 us -> 0 us
  Pallas kernels: 0 us -> 81.8 us
  between operations: 14.2 us -> 0.68 us
  matrix products: 11.6 us -> 0 us
  other arithmetic: 5.44 us -> 0.01 us
    psum x1 -> x0, waiting for transfers between devices: 242 us -> none  [local(): state, key_total = lax.psum((state_part, key_part), 'space')]
    psum x3 -> x0, blocking collectives: 242 us -> none  [the longest x1 136 us: local(): total_query, total_key = lax.psum((part_query, part_key), ('dp', 'space'))]
    pallas_call x0 -> x1, Pallas kernels: none -> 81.8 us  [local(): pl.pallas_call(run, out_shape=(big, big, big, jax.ShapeDtypeStruct((2, HE...]
    dot_general x8 -> x0, matrix products: 11.6 us -> none  [the longest x1 2.66 us: local(): jnp.einsum('hcd,hct->hdt', grad_state, feature_key, precision=highest)]
  transfers between devices with their start and end apart: 1 -> 0, of which waited for: 1 -> 0; matrix products, arithmetic and copies ran while one was open for 0% -> 0% of each run, Pallas kernels for 0% -> 0%
where the time goes in v1:
time: 91.7 us; the launch traced here: 91.4 us
  Pallas kernels  81.8 us (89%)
  local copies, waits for them, and re-layouts  8.86 us (10%)
    pallas_call x1, Pallas kernels, local(): pl.pallas_call(run, out_shape=(big, big, big, jax.ShapeDtypeStruct((2, HE...  81.8 us
    unnamed x13, local copies, waits for them, and re-layouts  6.66 us

profile of v1, /device:TPU:1, one launch (start us, length us, event | category | flops | bytes accessed | tf_op | source)
XLA Modules:
  0.0 91.4 jit_solution(14797773047699986142)
XLA Ops:
  0.6 0.0 copy-start.4
  0.6 0.8 reshape.16
  1.4 0.0 copy-done.4
  1.4 0.1 reshape.17
  1.5 0.0 copy-start
  1.5 1.1 %copy-done = bf16[1,1120,256]{2,1,0:T(8,128)(2,1)S(1)} copy-done((bf16[1,1120,256]{2,1,0:T(8,128)(2,1)S(1)}, bf16[1,1120,256]{2,1,0:T(8,128)(2,1)}, u32[]{:S(2)}) %copy-start) | copy-done | bytes 573464
  2.6 0.0 copy-start.1
  2.6 1.1 %copy-done.1 = bf16[1,1120,256]{2,1,0:T(8,128)(2,1)S(1)} copy-done((bf16[1,1120,256]{2,1,0:T(8,128)(2,1)S(1)}, bf16[1,1120,256]{2,1,0:T(8,128)(2,1)}, u32[]{:S(2)}) %copy-start.1) | copy-done | bytes 573464
  3.6 0.0 copy-start.2
  3.6 1.1 %copy-done.2 = bf16[1,1120,256]{2,1,0:T(8,128)(2,1)S(1)} copy-done((bf16[1,1120,256]{2,1,0:T(8,128)(2,1)S(1)}, bf16[1,1120,256]{2,1,0:T(8,128)(2,1)}, u32[]{:S(2)}) %copy-start.2) | copy-done | bytes 573464
  4.7 0.0 copy-start.3
  4.7 1.1 %copy-done.3 = bf16[1,1120,256]{2,1,0:T(8,128)(2,1)S(1)} copy-done((bf16[1,1120,256]{2,1,0:T(8,128)(2,1)S(1)}, bf16[1,1120,256]{2,1,0:T(8,128)(2,1)}, u32[]{:S(2)}) %copy-start.3) | copy-done | bytes 573464
  5.8 81.8 %linear_attention_backward.1 = (bf16[1,1120,256]{2,1,0:T(8,128)(2,1)S(1)}, bf16[1,1120,256]{2,1,0:T(8,128)(2,1)S(1)}, bf16[1,1120,256]{2,1,0:T(8,128)(2,1)S(1)}, f32[2,10,112]{2,1,0:T(8,128)S(1)}) custom-call(bf16[1,1120,256]{2,1,0:T(8,128)(2,1)S(1)} %copy-done, bf16[1,1120,256]{2,1,0:T(8,128)(2,1)S(1)} %copy-done.1, bf16[1,1120,256]{2,1,0:T(8,128)(2,1)S(1)} %copy-done.2, ...), custom_call_target="tpu_custom_call" | custom-call | tf_op jit(solution)/shard_map/linear_attention_backward/pallas_call | solution.py:447
  87.6 0.7 reshape_squeeze.7
  88.3 0.7 reshape_squeeze.6
  88.9 0.8 copy.14
  89.7 0.8 copy.15
  90.5 0.8 copy.16
  (2 shorter events, 0.0 us)
Async XLA Ops:
  0.6 0.8 copy-start.4
  1.5 1.1 %copy-start = (bf16[1,1120,256]{2,1,0:T(8,128)(2,1)S(1)}, bf16[1,1120,256]{2,1,0:T(8,128)(2,1)}, u32[]{:S(2)}) copy-start(bf16[1,1120,256]{2,1,0:T(8,128)(2,1)} %refs_0_.1) | copy-start | bytes 1720324
  2.6 1.1 %copy-start.1 = (bf16[1,1120,256]{2,1,0:T(8,128)(2,1)S(1)}, bf16[1,1120,256]{2,1,0:T(8,128)(2,1)}, u32[]{:S(2)}) copy-start(bf16[1,1120,256]{2,1,0:T(8,128)(2,1)} %refs_1_.1) | copy-start | bytes 1720324
  3.6 1.1 %copy-start.2 = (bf16[1,1120,256]{2,1,0:T(8,128)(2,1)S(1)}, bf16[1,1120,256]{2,1,0:T(8,128)(2,1)}, u32[]{:S(2)}) copy-start(bf16[1,1120,256]{2,1,0:T(8,128)(2,1)} %refs_2_.1) | copy-start | bytes 1720324
  4.7 1.1 %copy-start.3 = (bf16[1,1120,256]{2,1,0:T(8,128)(2,1)S(1)}, bf16[1,1120,256]{2,1,0:T(8,128)(2,1)}, u32[]{:S(2)}) copy-start(bf16[1,1120,256]{2,1,0:T(8,128)(2,1)} %refs_3_.1) | copy-start | bytes 1720324

commit v2 on v1

v2 whole, which is shorter than its diff:
```python
import math

import jax
import jax.numpy as jnp
from jax import lax
from jax.experimental import pallas as pl
from jax.experimental.pallas import tpu as pltpu
from jax.sharding import PartitionSpec as P

HEADS = 10
HEAD_DIM = 112
CH = HEADS * HEAD_DIM
LANES = 128
SPLIT_HEAD = 7
SPARE = LANES - HEAD_DIM
HOSTS = HEAD_DIM // SPARE
ROWS = 1024
PIECES = 4
PIECE = ROWS // PIECES
HALF = PIECE // 2
QUARTER = HALF // 4
OWN = QUARTER // 4
CLASS = PIECE // 4
KINDS = ("a", "a", "a", "b")
STAGES = 6
VMEM_BYTES = 62 << 20
CUTS = 2
Y, Z = 2, 16

norm_eps = 1e-06
denom_eps = 1e-06
F32 = jnp.float32
BF16 = jnp.bfloat16
MESH = pl.DeviceIdType.MESH
NT = (((1,), (1,)), ((), ()))
NN = (((1,), (0,)), ((), ()))
TN = (((0,), (0,)), ((), ()))


def dot(a, b, dims):
    return lax.dot_general(a, b, dims, preferred_element_type=F32)


def split(x):
    high = x.astype(BF16)
    return high, (x - high.astype(F32)).astype(BF16)


def rows_of(head):
    return pl.ds(head * HEAD_DIM, HEAD_DIM)


def block_of(head):
    return pl.ds((head if head < SPLIT_HEAD else head - 1) * HEAD_DIM, HEAD_DIM)


def kernel(
    clip_tokens,
    all_rows,
    dps,
    q_hbm,
    k_hbm,
    v_hbm,
    g_hbm,
    qg_hbm,
    kg_hbm,
    gq_hbm,
    gk_hbm,
    gv_hbm,
    gain_q_hbm,
    gain_k_hbm,
    q_in,
    k_in,
    v_in,
    g_in,
    qg_ref,
    kg_ref,
    gain_q_out,
    gain_k_out,
    feat_q,
    feat_k,
    inv_q,
    inv_k,
    rden,
    scaled_hi,
    scaled_lo,
    grad_f,
    out_q,
    out_k,
    out_v,
    gain_row,
    gain_col,
    kt_col,
    part,
    recv_y,
    half,
    recv_w,
    quarter,
    recv_s,
    full,
    one_a,
    one_b,
    two_a,
    two_b,
    three,
    sizes,
    load_sem,
    store_sem,
    send_sem,
    big_recv,
    small_recv,
    far_sem,
):
    tokens = q_in.shape[1]
    dp = lax.axis_index("dp")
    space = lax.axis_index("space")
    y, z = space // Z, space % Z
    k4, g4 = z % 4, z // 4
    sign = 1 - 2 * (dp % 2)

    def at(dy, dz):
        return (dp, lax.rem(y + dy, Y) * Z + lax.rem(z + dz + 2 * Z, Z))

    loads = [
        pltpu.make_async_copy(src, dst, load_sem.at[i])
        for i, (src, dst) in enumerate(
            (
                (k_hbm.at[0], k_in),
                (kg_hbm, kg_ref),
                (qg_hbm, qg_ref),
                (v_hbm.at[0], v_in),
                (q_hbm.at[0], q_in),
                (g_hbm.at[0], g_in),
            )
        )
    ]
    for load in loads:
        load.start()

    barrier = pltpu.get_barrier_semaphore()

    def cluster_peer(r):
        return (dp, lax.rem(y + r // 4, Y) * Z + g4 * 4 + lax.rem(k4 + r % 4, 4))

    greeted = 0
    for r in range(1, 8):
        pl.semaphore_signal(barrier, inc=1, device_id=cluster_peer(r), device_id_type=MESH)
        greeted += 1
    for dy, dz in ((0, 1), (0, -1), (0, 2), (0, -2), (0, 4), (0, -4), (1, 4), (1, -4)):
        pl.semaphore_signal(barrier, inc=1, device_id=at(dy, dz), device_id_type=MESH)
        greeted += 1
    for r in range(1, dps):
        pl.semaphore_signal(
            barrier, inc=1, device_id=(lax.rem(dp + r, dps), space), device_id_type=MESH
        )
        greeted += 1

    lane = lax.broadcasted_iota(jnp.int32, (HEAD_DIM, LANES), 1)
    ones = jnp.ones((16, tokens), BF16)
    no_rows = jnp.zeros((SPARE, tokens), BF16)

    def q_gain(h):
        return gain_col[0:HEAD_DIM, h : h + 1]

    def k_gain(h):
        return gain_col[0:HEAD_DIM, 16 + h : 17 + h]

    def pad(x):
        return jnp.concatenate([x, no_rows], axis=0)

    def features(x_in, inv_ref, gain, feat_ref, h):
        x = x_in[rows_of(h), :].astype(F32)
        inverse = lax.rsqrt(jnp.sum(x * x, axis=0, keepdims=True) * (1.0 / HEAD_DIM) + norm_eps)
        inv_ref[h : h + 1, :] = inverse
        feat = jnp.maximum((x * inverse) * gain(h), 0.0).astype(BF16)
        feat_ref[rows_of(h), :] = feat
        return feat

    def place(a, h, block, spread):
        if h < HOSTS:
            moved = pltpu.roll(spread, (HEAD_DIM - SPARE * h) % LANES, 1)
            block = jnp.where(lane >= HEAD_DIM, moved, block)
        part[a, block_of(h), :] = block

    def take(a, h):
        if h != SPLIT_HEAD:
            return full[a, block_of(h), :][:, 0:HEAD_DIM]
        whole = jnp.zeros((HEAD_DIM, LANES), F32)
        for j in range(HOSTS):
            moved = pltpu.roll(full[a, block_of(j), :], (SPARE * j - HEAD_DIM) % LANES, 1)
            whole = jnp.where((lane >= SPARE * j) & (lane < SPARE * (j + 1)), moved, whole)
        return whole[:, 0:HEAD_DIM]

    order = [SPLIT_HEAD] + [h for h in range(HEADS) if h != SPLIT_HEAD]
    tail = pl.ds((HEADS - 1) * HEAD_DIM, ROWS - (HEADS - 1) * HEAD_DIM)

    sent = [0]

    def go(recv_sem, copies):
        rows = 0
        for src, dst, peer in copies:
            pltpu.make_async_remote_copy(
                src_ref=src,
                dst_ref=dst,
                send_sem=send_sem,
                recv_sem=recv_sem,
                device_id=peer,
                device_id_type=MESH,
            ).start()
            rows += src.shape[0]
        sent[0] += rows
        return recv_sem, rows

    def wait_rows(sem, rows):
        ref = sizes.at[pl.ds(0, rows)]
        pltpu.make_async_copy(ref, ref, sem).wait()

    def land(came):
        wait_rows(*came)

    window = (sign, -sign, -2 * sign)
    stride = (4, 12, 8)
    both = [(r // 4, 4 * (r % 4)) for r in range(1, 8)]

    def near(start, size):
        return pl.ds(pl.multiple_of(start, size), size)

    def a_rs_y(a, p, came):
        src = part.at[a, near(p * PIECE + lax.rem(y + 1, Y) * HALF, HALF)]
        return go(big_recv.at[a, p, 0], [(src, recv_y.at[a, p], at(1, 0))])

    def a_rs_w(a, p, came):
        land(came)
        half[a, p] = part[a, near(p * PIECE + y * HALF, HALF), :] + recv_y[a, p]
        copies = []
        for m, dz in enumerate(window):
            src = half.at[a, p, near(lax.rem(z + dz + Z, 4) * QUARTER, QUARTER)]
            dst = recv_w.at[a, p, m, pl.ds(0, QUARTER)]
            copies.append((src, dst, at(0, dz)))
        return go(big_recv.at[a, p, 1], copies)

    def a_rs_s(a, p, came):
        land(came)
        cut = pl.ds(0, QUARTER)
        quarter[a, p, cut, :] = (
            half[a, p, near(k4 * QUARTER, QUARTER), :] + recv_w[a, p, 0, cut, :]
        ) + (recv_w[a, p, 1, cut, :] + recv_w[a, p, 2, cut, :])
        copies = []
        for m, dz in enumerate(stride):
            src = quarter.at[a, p, near(lax.rem(g4 + dz // 4, 4) * OWN, OWN)]
            copies.append((src, recv_s.at[a, p, m], at(0, dz)))
        return go(big_recv.at[a, p, 2], copies)

    def a_ag_s(a, p, came):
        land(came)
        own = near(p * PIECE + y * HALF + k4 * QUARTER + g4 * OWN, OWN)
        full[a, own, :] = (quarter[a, p, near(g4 * OWN, OWN), :] + recv_s[a, p, 0]) + (
            recv_s[a, p, 1] + recv_s[a, p, 2]
        )
        ref = full.at[a, own]
        return go(big_recv.at[a, p, 3], [(ref, ref, at(0, dz)) for dz in stride])

    def a_ag_w(a, p, came):
        land(came)
        ref = full.at[a, near(p * PIECE + y * HALF + k4 * QUARTER, QUARTER)]
        return go(big_recv.at[a, p, 4], [(ref, ref, at(0, dz)) for dz in window])

    def a_ag_y(a, p, came):
        land(came)
        ref = full.at[a, near(p * PIECE + y * HALF, HALF)]
        return go(big_recv.at[a, p, 5], [(ref, ref, at(1, 0))])

    def b_rs_w(a, p, came):
        copies = []
        for m, dz in enumerate(window):
            src = part.at[a, near(p * PIECE + lax.rem(z + dz + Z, 4) * CLASS, CLASS)]
            copies.append((src, recv_w.at[a, p, m], at(0, dz)))
        return go(big_recv.at[a, p, 0], copies)

    def b_rs_s(a, p, came):
        land(came)
        quarter[a, p] = (
            part[a, near(p * PIECE + k4 * CLASS, CLASS), :] + recv_w[a, p, 0]
        ) + (recv_w[a, p, 1] + recv_w[a, p, 2])
        copies = []
        for m, (dy, dz) in enumerate(both):
            start = lax.rem(y + dy, Y) * (4 * OWN) + lax.rem(g4 + dz // 4, 4) * OWN
            src = quarter.at[a, p, near(start, OWN)]
            copies.append((src, recv_s.at[a, p, m], at(dy, dz)))
        return go(big_recv.at[a, p, 1], copies)

    def b_ag_s(a, p, came):
        land(came)
        start = y * (4 * OWN) + g4 * OWN
        total = quarter[a, p, near(start, OWN), :]
        for m in range(len(both)):
            total = total + recv_s[a, p, m]
        own = near(p * PIECE + k4 * CLASS + start, OWN)
        full[a, own, :] = total
        ref = full.at[a, own]
        return go(big_recv.at[a, p, 2], [(ref, ref, at(dy, dz)) for dy, dz in both])

    def b_ag_w(a, p, came):
        land(came)
        ref = full.at[a, near(p * PIECE + k4 * CLASS, CLASS)]
        return go(big_recv.at[a, p, 3], [(ref, ref, at(0, dz)) for dz in window])

    stages = {
        "a": (a_rs_y, a_rs_w, a_rs_s, a_ag_s, a_ag_w, a_ag_y),
        "b": (b_rs_w, b_rs_s, b_ag_s, b_ag_w),
    }
    under_way = {}

    def step(a, *pieces):
        for p in pieces:
            at_stage, came = under_way.get((a, p), (0, None))
            todo = stages[KINDS[p]]
            if at_stage < len(todo):
                came = todo[at_stage](a, p, came)
            else:
                land(came)
            under_way[a, p] = (at_stage + 1, came)

    def small_cluster(slot, buf):
        ref = buf.at[y * 4 + k4]
        return go(small_recv.at[slot], [(ref, ref, cluster_peer(r)) for r in range(1, 8)])

    def small_stride(slot, came, buf_a, buf_b):
        land(came)
        total = buf_a[0]
        for e in range(1, 8):
            total = total + buf_a[e]
        buf_b[g4] = total
        ref = buf_b.at[g4]
        return go(small_recv.at[slot], [(ref, ref, at(0, dz)) for dz in stride])

    def small_done(came, buf_b):
        land(came)
        return (buf_b[0] + buf_b[1]) + (buf_b[2] + buf_b[3])

    cell = y * 4 + k4
    one_a[cell] = jnp.zeros_like(one_a[cell])
    two_a[cell] = jnp.zeros_like(two_a[cell])
    part[0, tail, :] = jnp.zeros((tail.size, LANES), F32)
    part[1, tail, :] = jnp.zeros((tail.size, LANES), F32)

    def after(p):
        done = []
        for h in order[1:]:
            last = block_of(h).start + HEAD_DIM - 1
            if min(last // PIECE, PIECES - 1) == p:
                done.append(h)
        return done

    pieces = range(PIECES)
    A = [p for p in pieces if KINDS[p] == "a"]
    B = [p for p in pieces if KINDS[p] == "b"]

    def state_blocks(p, spread):
        for h in ([SPLIT_HEAD] if p == 0 else []) + ready[p]:
            block = dot(feat_k[rows_of(h), :], pad(v_in[rows_of(h), :]), NT)
            if h == SPLIT_HEAD:
                spread = block
            else:
                place(0, h, block, spread)
        return spread

    ready = []
    for p in pieces:
        ready.append(
            [
                h
                for h in order[1:]
                if (p - 1 if p else -1) * PIECE + PIECE <= block_of(h).start < (p + 1) * PIECE
            ]
        )

    for load in loads[:3]:
        load.wait()
    gain_row[...] = jnp.ones_like(gain_row)
    for h in range(HEADS):
        cut = pl.ds(h * HEAD_DIM, HEAD_DIM)
        gain_row[h, 0:HEAD_DIM] = qg_ref[cut]
        gain_row[16 + h, 0:HEAD_DIM] = kg_ref[cut]
    gain_col[...] = jnp.transpose(gain_row[...])
    for h in range(HEADS):
        feat = features(k_in, inv_k, k_gain, feat_k, h)
        one_a[cell, h : h + 1, 0:HEAD_DIM] = dot(ones, feat, NT)[0:1]
    pl.semaphore_wait(barrier, greeted)
    pl.semaphore_signal(far_sem, inc=1, device_id=at(0, 4), device_id_type=MESH)
    ar1 = small_cluster(0, one_a)
    loads[3].wait()
    spread = None
    for p in pieces:
        spread = state_blocks(p, spread)
        step(0, p)
    loads[4].wait()
    for h in range(HEADS):
        features(q_in, inv_q, q_gain, feat_q, h)
    pl.semaphore_wait(far_sem, 1)
    ar1 = small_stride(1, ar1, one_a, one_b)
    step(0, *A, *B, *A)

    loads[5].wait()
    key_total = small_done(ar1, one_b)
    kt_col[...] = jnp.transpose(key_total)
    kt_hi, kt_mid = split(key_total)
    kt_lo = (key_total - kt_hi.astype(F32) - kt_mid.astype(F32)).astype(BF16)
    kt3 = jnp.concatenate([kt_hi, kt_mid, kt_lo], axis=0)[:, 0:HEAD_DIM]
    loss_scale = math.sqrt(clip_tokens)

    def grad_state_blocks(p, spread):
        for h in ([SPLIT_HEAD] if p == 0 else []) + ready[p]:
            feat = feat_q[rows_of(h), :]
            terms = dot(kt3, feat, NN)
            denominator = (
                terms[h : h + 1] + (terms[16 + h : 17 + h] + terms[32 + h : 33 + h])
            ) + denom_eps
            inverse = 1.0 / denominator
            rden[h : h + 1, :] = inverse
            scaled = g_in[rows_of(h), :].astype(F32) * (loss_scale * inverse)
            high, low = split(scaled)
            scaled_hi[rows_of(h), :] = high
            scaled_lo[rows_of(h), :] = low
            block = dot(feat, pad(high), NT) + dot(feat, pad(low), NT)
            if h == SPLIT_HEAD:
                spread = block
            else:
                place(1, h, block, spread)
        return spread

    for p in pieces:
        spread = grad_state_blocks(p, spread)
        step(1, p)
    step(1, *A)
    step(0, *B, *A)
    step(1, *B, *A)
    step(0, *B, *A, *A)

    def query_head(h):
        feat = feat_q[rows_of(h), :]
        high, low = scaled_hi[rows_of(h), :], scaled_lo[rows_of(h), :]
        state_hi, state_lo = split(take(0, h))
        grad = dot(state_hi, high, NN) + (dot(state_lo, high, NN) + dot(state_hi, low, NN))
        feat_f = feat.astype(F32)
        projected = jnp.sum(feat_f * grad, axis=0, keepdims=True) * rden[h : h + 1, :]
        grad = grad - kt_col[0:HEAD_DIM, h : h + 1] * projected
        grad_f[rows_of(h), :] = grad
        p_hi, p_lo = split(-projected)
        two_a[cell, HEADS + h : HEADS + h + 1, 0:HEAD_DIM] = (
            dot(jnp.broadcast_to(p_hi, (16, tokens)), feat, NT)
            + dot(jnp.broadcast_to(p_lo, (16, tokens)), feat, NT)
        )[0:1]
        e_hi, e_lo = split(feat_f * grad)
        two_a[cell, h : h + 1, 0:HEAD_DIM] = (
            dot(ones, e_hi, NT) + dot(ones, e_lo, NT)
        )[0:1]

    arrives = [[h for h in after(p)] for p in pieces]
    arrives[-1].append(SPLIT_HEAD)

    for p in pieces:
        step(0, p)
        for h in arrives[p]:
            query_head(h)
    ar2 = small_cluster(2, two_a)
    step(1, *A, *B)

    def norm_backward(x_in, inv_ref, gain, feat, grad, out, h):
        inverse = inv_ref[h : h + 1, :]
        unit = x_in[rows_of(h), :].astype(F32) * inverse
        upstream = jnp.where(feat > 0, grad, 0.0) * gain(h)
        mean = jnp.sum(upstream * unit, axis=0, keepdims=True) * (1.0 / HEAD_DIM)
        out[rows_of(h), :] = (inverse * (upstream - unit * mean)).astype(BF16)

    def grad_queries(heads):
        for h in heads:
            feat = feat_q[rows_of(h), :].astype(F32)
            norm_backward(q_in, inv_q, q_gain, feat, grad_f[rows_of(h), :], out_q, h)

    grad_queries(range(0, 5))
    ar2 = small_stride(3, ar2, two_a, two_b)
    step(1, *A, *B)
    grad_queries(range(5, HEADS))
    store_q = pltpu.make_async_copy(out_q, gq_hbm.at[0], store_sem.at[0])
    store_q.start()
    step(1, *A)

    total = small_done(ar2, two_b)
    three[dp] = total[0:16]
    ref = three.at[dp]
    ar3 = go(
        small_recv.at[4], [(ref, ref, (lax.rem(dp + r, dps), space)) for r in range(1, dps)]
    )

    for p in pieces:
        step(1, p)
        for h in arrives[p]:
            gs_hi, gs_lo = split(take(1, h))
            value = v_in[rows_of(h), :]
            feat = feat_k[rows_of(h), :]
            out_v[rows_of(h), :] = (dot(gs_hi, feat, TN) + dot(gs_lo, feat, TN)).astype(BF16)
            grad_f[rows_of(h), :] = dot(gs_hi, value, NN) + dot(gs_lo, value, NN)
    store_v = pltpu.make_async_copy(out_v, gv_hbm.at[0], store_sem.at[1])
    store_v.start()

    gkt_col = jnp.transpose(total)
    for h in range(HEADS):
        feat = feat_k[rows_of(h), :].astype(F32)
        grad = grad_f[rows_of(h), :] + gkt_col[0:HEAD_DIM, HEADS + h : HEADS + h + 1]
        norm_backward(k_in, inv_k, k_gain, feat, grad, out_k, h)
    store_k = pltpu.make_async_copy(out_k, gk_hbm.at[0], store_sem.at[2])
    store_k.start()

    land(ar3)
    total = three[0]
    for r in range(1, dps):
        total = total + three[r]
    gain_sum = total[0:HEADS, 0:HEAD_DIM] * (1.0 / math.sqrt(all_rows))
    grad_q_gain = gain_sum / gain_row[0:HEADS, 0:HEAD_DIM]
    grad_k_gain = gain_sum / gain_row[16 : 16 + HEADS, 0:HEAD_DIM]
    for h in range(HEADS):
        cut = pl.ds(h * HEAD_DIM, HEAD_DIM)
        gain_q_out[cut] = grad_q_gain[h]
        gain_k_out[cut] = grad_k_gain[h]
    store_gains = [
        pltpu.make_async_copy(gain_q_out, gain_q_hbm, store_sem.at[3]),
        pltpu.make_async_copy(gain_k_out, gain_k_hbm, store_sem.at[4]),
    ]
    for store in store_gains:
        store.start()

    wait_rows(send_sem, sent[0])
    for store in (store_q, store_v, store_k, *store_gains):
        store.wait()


def hand_over(*refs):
    sources, results, held, load_sem, store_sem = refs[:3], refs[3:6], *refs[6:]
    rows = CH // CUTS
    loads, stores = [], []
    for i, (src, dst) in enumerate(zip(sources, results)):
        for part in range(CUTS):
            cut = pl.ds(part * rows, rows)
            n = i * CUTS + part
            loads.append(pltpu.make_async_copy(src.at[0, cut], held.at[i, cut], load_sem.at[n]))
            stores.append(pltpu.make_async_copy(held.at[i, cut], dst.at[0, cut], store_sem.at[n]))
    for load in loads:
        load.start()
    for load, store in zip(loads, stores):
        load.wait()
        store.start()
    for store in stores:
        store.wait()


def local(queries, keys, values, out_grad, q_gain, k_gain):
    tokens = queries.shape[2]
    dps = lax.axis_size("dp")
    clip_tokens = tokens * lax.axis_size("space")
    all_rows = clip_tokens * dps * queries.shape[0]
    anywhere = pl.BlockSpec(memory_space=pl.ANY)
    big = jax.ShapeDtypeStruct(queries.shape, BF16)
    row = jax.ShapeDtypeStruct((CH,), F32)
    vm = pltpu.VMEM
    dma = pltpu.SemaphoreType.DMA

    def run(*refs):
        kernel(clip_tokens, all_rows, dps, *refs)

    *grads, gain_q, gain_k = pl.pallas_call(
        run,
        out_shape=(big, big, big, row, row),
        in_specs=[anywhere] * 6,
        out_specs=(anywhere,) * 5,
        scratch_shapes=[
            vm((CH, tokens), BF16),
            vm((CH, tokens), BF16),
            vm((CH, tokens), BF16),
            vm((CH, tokens), BF16),
            vm((CH,), F32),
            vm((CH,), F32),
            vm((CH,), F32),
            vm((CH,), F32),
            vm((CH, tokens), BF16),
            vm((CH, tokens), BF16),
            vm((16, tokens), F32),
            vm((16, tokens), F32),
            vm((16, tokens), F32),
            vm((CH, tokens), BF16),
            vm((CH, tokens), BF16),
            vm((CH, tokens), F32),
            vm((CH, tokens), BF16),
            vm((CH, tokens), BF16),
            vm((CH, tokens), BF16),
            vm((32, LANES), F32),
            vm((LANES, 32), F32),
            vm((LANES, 16), F32),
            vm((2, ROWS, LANES), F32),
            vm((2, PIECES, HALF, LANES), F32),
            vm((2, PIECES, HALF, LANES), F32),
            vm((2, PIECES, 3, CLASS, LANES), F32),
            vm((2, PIECES, CLASS, LANES), F32),
            vm((2, PIECES, 7, OWN, LANES), F32),
            vm((2, ROWS, LANES), F32),
            vm((8, 16, LANES), F32),
            vm((4, 16, LANES), F32),
            vm((8, 24, LANES), F32),
            vm((4, 24, LANES), F32),
            vm((dps, 16, LANES), F32),
            vm((2 * 2048 + 640, LANES), F32),
            dma((6,)),
            dma((5,)),
            dma(()),
            dma((2, PIECES, STAGES)),
            dma((5,)),
            pltpu.SemaphoreType.REGULAR,
        ],
        compiler_params=pltpu.CompilerParams(
            collective_id=0, has_side_effects=True, vmem_limit_bytes=VMEM_BYTES
        ),
        name="linear_attention_backward",
    )(queries, keys, values, out_grad, q_gain, k_gain)
    grads = pl.pallas_call(
        hand_over,
        out_shape=(big, big, big),
        in_specs=[anywhere] * 3,
        out_specs=(anywhere,) * 3,
        scratch_shapes=[vm((3, CH, tokens), BF16), dma((3 * CUTS,)), dma((3 * CUTS,))],
        compiler_params=pltpu.CompilerParams(vmem_limit_bytes=VMEM_BYTES),
        name="hand_over",
    )(*grads)
    return (*grads, gain_q, gain_k)


def solution(mesh):
    whole = P("dp", None, "space")
    return jax.shard_map(
        local,
        mesh=mesh,
        in_specs=(whole, whole, whole, whole, P(), P()),
        out_specs=(whole, whole, whole, P(), P()),
        check_vma=False,
    )
```

time: 91.7 us -> 80.2 us (0.87)
  local copies, waits for them, and re-layouts: 8.86 us -> 1.29 us
  Pallas kernels: 81.8 us -> 78 us
    unnamed x13 -> x6, local copies, waits for them, and re-layouts: 6.66 us -> 1.29 us
    pallas_call x1 -> x2, Pallas kernels: 81.8 us -> 78 us  [the longest x1 75.8 us: local(): pl.pallas_call(run, out_shape=(big, big, big, row, row), in_specs=[anywhe...]
    another operation x2 -> x0, local copies, waits for them, and re-layouts: 1.35 us -> none  [the longest x1 0.67 us: local(): gain_grads[1].reshape(CH)]
where the time goes in v2:
time: 80.2 us; the launch traced here: 80 us
  Pallas kernels  78 us (97%)
  local copies, waits for them, and re-layouts  1.29 us (2%)
    pallas_call x1, Pallas kernels, local(): pl.pallas_call(run, out_shape=(big, big, big, row, row), in_specs=[anywhe...  75.8 us
    pallas_call x1, Pallas kernels, local(): pl.pallas_call(hand_over, out_shape=(big, big, big), in_specs=[anywhere]...  2.25 us

profile of v2, /device:TPU:1, one launch (start us, length us, event | category | flops | bytes accessed | tf_op | source)
XLA Modules:
  0.0 80.0 jit_solution(8295947103397046127)
XLA Ops:
  0.6 75.8 %linear_attention_backward.1 = (bf16[1,1120,256]{2,1,0:T(8,128)(2,1)}, bf16[1,1120,256]{2,1,0:T(8,128)(2,1)}, bf16[1,1120,256]{2,1,0:T(8,128)(2,1)}, f32[1120]{0:T(1024)}, f32[1120]{0:T(1024)}) custom-call(bf16[1,1120,256]{2,1,0:T(8,128)(2,1)} %refs_0_.1, bf16[1,1120,256]{2,1,0:T(8,128)(2,1)} %refs_1_.1, bf16[1,1120,256]{2,1,0:T(8,128)(2,1)} %refs_2_.1, ...), custom_call_target="tpu_custom_call" | custom-call | tf_op jit(solution)/shard_map/linear_attention_backward/pallas_call | solution.py:571
  76.4 0.0 copy-start.1
  76.4 2.3 %hand_over.1 = (bf16[1,1120,256]{2,1,0:T(8,128)(2,1)}, bf16[1,1120,256]{2,1,0:T(8,128)(2,1)}, bf16[1,1120,256]{2,1,0:T(8,128)(2,1)}) custom-call(bf16[1,1120,256]{2,1,0:T(8,128)(2,1)} %get-tuple-element.13.refs_0_, bf16[1,1120,256]{2,1,0:T(8,128)(2,1)} %get-tuple-element.14.refs_1_, bf16[1,1120,256]{2,1,0:T(8,128)(2,1)} %get-tuple-element.15.refs_2_), custom_call_target="tpu_custom_call" | custom-call | tf_op jit(solution)/shard_map/hand_over/pallas_call | solution.py:624
  78.7 0.0 copy-done.1
  78.7 0.0 copy-start
  78.7 0.6 copy.13
  79.3 0.1 copy-done
  79.4 0.6 copy.14
Async XLA Ops:
  76.4 2.3 %copy-start.1 = (f32[1120]{0:T(1024)S(1)}, f32[1120]{0:T(1024)}, u32[]{:S(2)}) copy-start(f32[1120]{0:T(1024)} %get-tuple-element.29) | copy-start | bytes 13444
  78.7 0.7 copy-start

commit v3 on v2

--- a/solution.py
+++ b/solution.py
@@ -18,11 +18,15 @@
 PIECES = 4
 PIECE = ROWS // PIECES
 HALF = PIECE // 2
-QUARTER = HALF // 4
-OWN = QUARTER // 4
-CLASS = PIECE // 4
-KINDS = ("a", "a", "a", "b")
+OWN = HALF // 16
 STAGES = 6
+SPOTS = (-1, -3, -6, 1, 3, 6, -2, -4, -7, -5, -8, 2, 4, 7, 5, 0)
+COLLECT = 6
+STAGE_AT = (0.0, 3.0, 6.2, 11.7, 17.0, 20.0, 23.2)
+PIECE_GAP = 1.3
+GRAD_LAG = 10.4
+OPPOSITE = (3, 4, 5, 0, 1, 2)
+HANDS = ((-1, 6, 9, 0), (-2, 9, 11, 1), (1, 11, 14, 3), (2, 14, 15, 4))
 VMEM_BYTES = 62 << 20
 CUTS = 2
 Y, Z = 2, 16
@@ -95,8 +99,8 @@
     recv_y,
     half,
     recv_w,
-    quarter,
     recv_s,
+    held,
     full,
     one_a,
     one_b,
@@ -146,7 +150,7 @@
     for r in range(1, 8):
         pl.semaphore_signal(barrier, inc=1, device_id=cluster_peer(r), device_id_type=MESH)
         greeted += 1
-    for dy, dz in ((0, 1), (0, -1), (0, 2), (0, -2), (0, 4), (0, -4), (1, 4), (1, -4)):
+    for dy, dz in ((0, 1), (0, -1), (0, 2), (0, -2), (0, 3), (0, -3), (0, 4), (0, -4)):
         pl.semaphore_signal(barrier, inc=1, device_id=at(dy, dz), device_id_type=MESH)
         greeted += 1
     for r in range(1, dps):
@@ -218,107 +222,97 @@
     def land(came):
         wait_rows(*came)
 
-    window = (sign, -sign, -2 * sign)
     stride = (4, 12, 8)
-    both = [(r // 4, 4 * (r % 4)) for r in range(1, 8)]
 
     def near(start, size):
         return pl.ds(pl.multiple_of(start, size), size)
 
-    def a_rs_y(a, p, came):
+    def owner_rows(spot):
+        return lax.rem(z + SPOTS[spot] * sign + Z, Z) * OWN
+
+    def spots(first, last):
+        return pl.ds(first * OWN, (last - first) * OWN)
+
+    def rs_y(a, p, came):
         src = part.at[a, near(p * PIECE + lax.rem(y + 1, Y) * HALF, HALF)]
         return go(big_recv.at[a, p, 0], [(src, recv_y.at[a, p], at(1, 0))])
 
-    def a_rs_w(a, p, came):
+    def rs_w(a, p, came):
         land(came)
-        half[a, p] = part[a, near(p * PIECE + y * HALF, HALF), :] + recv_y[a, p]
+        base = p * PIECE + y * HALF
+        for spot in range(16):
+            rows = owner_rows(spot)
+            half[a, p, pl.ds(spot * OWN, OWN), :] = (
+                part[a, near(base + rows, OWN), :] + recv_y[a, p, near(rows, OWN), :]
+            )
+        copies, filled = [], 0
+        for dz, first, last, _ in HANDS:
+            dst = recv_w.at[a, p, spots(filled, filled + last - first)]
+            copies.append((half.at[a, p, spots(first, last)], dst, at(0, dz * sign)))
+            filled += last - first
+        return go(big_recv.at[a, p, 1], copies)
+
+    def rs_s(a, p, came):
+        land(came)
+        filled = 0
+        for dz, first, last, to in HANDS:
+            count = last - first
+            mine = spots(to, to + count)
+            half[a, p, mine, :] = half[a, p, mine, :] + recv_w[a, p, spots(filled, filled + count), :]
+            filled += count
+        return go(
+            big_recv.at[a, p, 2],
+            [
+                (half.at[a, p, spots(i, i + 1)], recv_s.at[a, p, i], at(0, SPOTS[i] * sign))
+                for i in range(COLLECT)
+            ],
+        )
+
+    def ag_s(a, p, came):
+        land(came)
+        own = spots(15, 16)
+        total = half[a, p, own, :]
+        for i in range(COLLECT):
+            total = total + recv_s[a, p, i]
+        held[a, p, 0, own, :] = total
+        return go(
+            big_recv.at[a, p, 3],
+            [
+                (held.at[a, p, 0, own], held.at[a, p, 0, spots(OPPOSITE[i], OPPOSITE[i] + 1)], at(0, SPOTS[i] * sign))
+                for i in range(COLLECT)
+            ],
+        )
+
+    def ag_w(a, p, came):
+        land(came)
         copies = []
-        for m, dz in enumerate(window):
-            src = half.at[a, p, near(lax.rem(z + dz + Z, 4) * QUARTER, QUARTER)]
-            dst = recv_w.at[a, p, m, pl.ds(0, QUARTER)]
-            copies.append((src, dst, at(0, dz)))
-        return go(big_recv.at[a, p, 1], copies)
-
-    def a_rs_s(a, p, came):
+        for dz, first, last, to in HANDS:
+            src = held.at[a, p, 0, spots(to, to + last - first)]
+            copies.append((src, held.at[a, p, 0, spots(first, last)], at(0, -dz * sign)))
+        return go(big_recv.at[a, p, 4], copies)
+
+    def ag_y(a, p, came):
         land(came)
-        cut = pl.ds(0, QUARTER)
-        quarter[a, p, cut, :] = (
-            half[a, p, near(k4 * QUARTER, QUARTER), :] + recv_w[a, p, 0, cut, :]
-        ) + (recv_w[a, p, 1, cut, :] + recv_w[a, p, 2, cut, :])
-        copies = []
-        for m, dz in enumerate(stride):
-            src = quarter.at[a, p, near(lax.rem(g4 + dz // 4, 4) * OWN, OWN)]
-            copies.append((src, recv_s.at[a, p, m], at(0, dz)))
-        return go(big_recv.at[a, p, 2], copies)
-
-    def a_ag_s(a, p, came):
-        land(came)
-        own = near(p * PIECE + y * HALF + k4 * QUARTER + g4 * OWN, OWN)
-        full[a, own, :] = (quarter[a, p, near(g4 * OWN, OWN), :] + recv_s[a, p, 0]) + (
-            recv_s[a, p, 1] + recv_s[a, p, 2]
-        )
-        ref = full.at[a, own]
-        return go(big_recv.at[a, p, 3], [(ref, ref, at(0, dz)) for dz in stride])
-
-    def a_ag_w(a, p, came):
-        land(came)
-        ref = full.at[a, near(p * PIECE + y * HALF + k4 * QUARTER, QUARTER)]
-        return go(big_recv.at[a, p, 4], [(ref, ref, at(0, dz)) for dz in window])
-
-    def a_ag_y(a, p, came):
-        land(came)
-        ref = full.at[a, near(p * PIECE + y * HALF, HALF)]
-        return go(big_recv.at[a, p, 5], [(ref, ref, at(1, 0))])
-
-    def b_rs_w(a, p, came):
-        copies = []
-        for m, dz in enumerate(window):
-            src = part.at[a, near(p * PIECE + lax.rem(z + dz + Z, 4) * CLASS, CLASS)]
-            copies.append((src, recv_w.at[a, p, m], at(0, dz)))
-        return go(big_recv.at[a, p, 0], copies)
-
-    def b_rs_s(a, p, came):
-        land(came)
-        quarter[a, p] = (
-            part[a, near(p * PIECE + k4 * CLASS, CLASS), :] + recv_w[a, p, 0]
-        ) + (recv_w[a, p, 1] + recv_w[a, p, 2])
-        copies = []
-        for m, (dy, dz) in enumerate(both):
-            start = lax.rem(y + dy, Y) * (4 * OWN) + lax.rem(g4 + dz // 4, 4) * OWN
-            src = quarter.at[a, p, near(start, OWN)]
-            copies.append((src, recv_s.at[a, p, m], at(dy, dz)))
-        return go(big_recv.at[a, p, 1], copies)
-
-    def b_ag_s(a, p, came):
-        land(came)
-        start = y * (4 * OWN) + g4 * OWN
-        total = quarter[a, p, near(start, OWN), :]
-        for m in range(len(both)):
-            total = total + recv_s[a, p, m]
-        own = near(p * PIECE + k4 * CLASS + start, OWN)
-        full[a, own, :] = total
-        ref = full.at[a, own]
-        return go(big_recv.at[a, p, 2], [(ref, ref, at(dy, dz)) for dy, dz in both])
-
-    def b_ag_w(a, p, came):
-        land(came)
-        ref = full.at[a, near(p * PIECE + k4 * CLASS, CLASS)]
-        return go(big_recv.at[a, p, 3], [(ref, ref, at(0, dz)) for dz in window])
-
-    stages = {
-        "a": (a_rs_y, a_rs_w, a_rs_s, a_ag_s, a_ag_w, a_ag_y),
-        "b": (b_rs_w, b_rs_s, b_ag_s, b_ag_w),
-    }
+        came = go(big_recv.at[a, p, 5], [(held.at[a, p, 0], held.at[a, p, 1], at(1, 0))])
+        spread_out(a, p, 0, y)
+        return came
+
+    def spread_out(a, p, which, side):
+        for spot in range(16):
+            rows = near(p * PIECE + side * HALF + owner_rows(spot), OWN)
+            full[a, rows, :] = held[a, p, which, pl.ds(spot * OWN, OWN), :]
+
+    todo = (rs_y, rs_w, rs_s, ag_s, ag_w, ag_y)
     under_way = {}
 
     def step(a, *pieces):
         for p in pieces:
             at_stage, came = under_way.get((a, p), (0, None))
-            todo = stages[KINDS[p]]
             if at_stage < len(todo):
                 came = todo[at_stage](a, p, came)
             else:
                 land(came)
+                spread_out(a, p, 1, lax.rem(y + 1, Y))
             under_way[a, p] = (at_stage + 1, came)
 
     def small_cluster(slot, buf):
@@ -353,8 +347,8 @@
         return done
 
     pieces = range(PIECES)
-    A = [p for p in pieces if KINDS[p] == "a"]
-    B = [p for p in pieces if KINDS[p] == "b"]
+    A = list(pieces)
+    B = []
 
     def state_blocks(p, spread):
         for h in ([SPLIT_HEAD] if p == 0 else []) + ready[p]:
@@ -387,7 +381,8 @@
         feat = features(k_in, inv_k, k_gain, feat_k, h)
         one_a[cell, h : h + 1, 0:HEAD_DIM] = dot(ones, feat, NT)[0:1]
     pl.semaphore_wait(barrier, greeted)
-    pl.semaphore_signal(far_sem, inc=1, device_id=at(0, 4), device_id_type=MESH)
+    for dz in (4, -4):
+        pl.semaphore_signal(far_sem, inc=1, device_id=at(0, dz), device_id_type=MESH)
     ar1 = small_cluster(0, one_a)
     loads[3].wait()
     spread = None
@@ -397,9 +392,10 @@
     loads[4].wait()
     for h in range(HEADS):
         features(q_in, inv_q, q_gain, feat_q, h)
-    pl.semaphore_wait(far_sem, 1)
+    step(0, 0)
+    pl.semaphore_wait(far_sem, 2)
     ar1 = small_stride(1, ar1, one_a, one_b)
-    step(0, *A, *B, *A)
+    step(0, 1, 2, 3, 0, 1, 2, 3)
 
     loads[5].wait()
     key_total = small_done(ar1, one_b)
@@ -432,10 +428,6 @@
     for p in pieces:
         spread = grad_state_blocks(p, spread)
         step(1, p)
-    step(1, *A)
-    step(0, *B, *A)
-    step(1, *B, *A)
-    step(0, *B, *A, *A)
 
     def query_head(h):
         feat = feat_q[rows_of(h), :]
@@ -459,12 +451,20 @@
     arrives = [[h for h in after(p)] for p in pieces]
     arrives[-1].append(SPLIT_HEAD)
 
-    for p in pieces:
-        step(0, p)
-        for h in arrives[p]:
-            query_head(h)
+    last = len(todo)
+    order_of_steps = sorted(
+        (STAGE_AT[k] + PIECE_GAP * p + GRAD_LAG * a, a, p, k)
+        for a, first in ((0, 3), (1, 1))
+        for p in pieces
+        for k in range(first, last + 1)
+    )
+    end = order_of_steps.index((STAGE_AT[last] + PIECE_GAP * (PIECES - 1), 0, PIECES - 1, last))
+    for _, a, p, k in order_of_steps[: end + 1]:
+        step(a, p)
+        if a == 0 and k == last:
+            for h in arrives[p]:
+                query_head(h)
     ar2 = small_cluster(2, two_a)
-    step(1, *A, *B)
 
     def norm_backward(x_in, inv_ref, gain, feat, grad, out, h):
         inverse = inv_ref[h : h + 1, :]
@@ -478,20 +478,21 @@
             feat = feat_q[rows_of(h), :].astype(F32)
             norm_backward(q_in, inv_q, q_gain, feat, grad_f[rows_of(h), :], out_q, h)
 
+    rest = [(p, k) for _, a, p, k in order_of_steps[end + 1 :]]
+
+    def go_on(stage):
+        for p, k in rest:
+            if k == stage:
+                step(1, p)
+
+    go_on(3)
     grad_queries(range(0, 5))
+    go_on(4)
     ar2 = small_stride(3, ar2, two_a, two_b)
-    step(1, *A, *B)
     grad_queries(range(5, HEADS))
     store_q = pltpu.make_async_copy(out_q, gq_hbm.at[0], store_sem.at[0])
     store_q.start()
-    step(1, *A)
-
-    total = small_done(ar2, two_b)
-    three[dp] = total[0:16]
-    ref = three.at[dp]
-    ar3 = go(
-        small_recv.at[4], [(ref, ref, (lax.rem(dp + r, dps), space)) for r in range(1, dps)]
-    )
+    go_on(5)
 
     for p in pieces:
         step(1, p)
@@ -503,6 +504,13 @@
             grad_f[rows_of(h), :] = dot(gs_hi, value, NN) + dot(gs_lo, value, NN)
     store_v = pltpu.make_async_copy(out_v, gv_hbm.at[0], store_sem.at[1])
     store_v.start()
+
+    total = small_done(ar2, two_b)
+    three[dp] = total[0:16]
+    ref = three.at[dp]
+    ar3 = go(
+        small_recv.at[4], [(ref, ref, (lax.rem(dp + r, dps), space)) for r in range(1, dps)]
+    )
 
     gkt_col = jnp.transpose(total)
     for h in range(HEADS):
@@ -599,9 +607,9 @@
             vm((2, ROWS, LANES), F32),
             vm((2, PIECES, HALF, LANES), F32),
             vm((2, PIECES, HALF, LANES), F32),
-            vm((2, PIECES, 3, CLASS, LANES), F32),
-            vm((2, PIECES, CLASS, LANES), F32),
-            vm((2, PIECES, 7, OWN, LANES), F32),
+            vm((2, PIECES, 9 * OWN, LANES), F32),
+            vm((2, PIECES, COLLECT, OWN, LANES), F32),
+            vm((2, PIECES, 2, HALF, LANES), F32),
             vm((2, ROWS, LANES), F32),
             vm((8, 16, LANES), F32),
             vm((4, 16, LANES), F32),

time: 80.2 us -> 74 us (0.923)
  Pallas kernels: 78 us -> 71.8 us
    pallas_call x1, Pallas kernels: 75.8 us -> 69.6 us  [local(): pl.pallas_call(run, out_shape=(big, big, big, row, row), in_specs=[anywhe...]
where the time goes in v3:
time: 74 us; the launch traced here: 73.8 us
  Pallas kernels  71.8 us (97%)
  local copies, waits for them, and re-layouts  1.29 us (2%)
    pallas_call x1, Pallas kernels, local(): pl.pallas_call(run, out_shape=(big, big, big, row, row), in_specs=[anywhe...  69.6 us
    pallas_call x1, Pallas kernels, local(): pl.pallas_call(hand_over, out_shape=(big, big, big), in_specs=[anywhere]...  2.25 us

profile of v3, /device:TPU:1, one launch (start us, length us, event | category | flops | bytes accessed | tf_op | source)
XLA Modules:
  0.0 73.8 jit_solution(10127331803632616239)
XLA Ops:
  0.6 69.6 %linear_attention_backward.1 = (bf16[1,1120,256]{2,1,0:T(8,128)(2,1)}, bf16[1,1120,256]{2,1,0:T(8,128)(2,1)}, bf16[1,1120,256]{2,1,0:T(8,128)(2,1)}, f32[1120]{0:T(1024)}, f32[1120]{0:T(1024)}) custom-call(bf16[1,1120,256]{2,1,0:T(8,128)(2,1)} %refs_0_.1, bf16[1,1120,256]{2,1,0:T(8,128)(2,1)} %refs_1_.1, bf16[1,1120,256]{2,1,0:T(8,128)(2,1)} %refs_2_.1, ...), custom_call_target="tpu_custom_call" | custom-call | tf_op jit(solution)/shard_map/linear_attention_backward/pallas_call | solution.py:579
  70.2 0.0 copy-start.1
  70.2 2.3 %hand_over.1 = (bf16[1,1120,256]{2,1,0:T(8,128)(2,1)}, bf16[1,1120,256]{2,1,0:T(8,128)(2,1)}, bf16[1,1120,256]{2,1,0:T(8,128)(2,1)}) custom-call(bf16[1,1120,256]{2,1,0:T(8,128)(2,1)} %get-tuple-element.13.refs_0_, bf16[1,1120,256]{2,1,0:T(8,128)(2,1)} %get-tuple-element.14.refs_1_, bf16[1,1120,256]{2,1,0:T(8,128)(2,1)} %get-tuple-element.15.refs_2_), custom_call_target="tpu_custom_call" | custom-call | tf_op jit(solution)/shard_map/hand_over/pallas_call | solution.py:632
  72.5 0.0 copy-done.1
  72.5 0.0 copy-start
  72.5 0.6 copy.13
  73.1 0.1 copy-done
  73.2 0.6 copy.14
Async XLA Ops:
  70.2 2.3 %copy-start.1 = (f32[1120]{0:T(1024)S(1)}, f32[1120]{0:T(1024)}, u32[]{:S(2)}) copy-start(f32[1120]{0:T(1024)} %get-tuple-element.29) | copy-start | bytes 13444
  72.5 0.7 copy-start

commit v4 on v3

--- a/solution.py
+++ b/solution.py
@@ -23,12 +23,11 @@
 SPOTS = (-1, -3, -6, 1, 3, 6, -2, -4, -7, -5, -8, 2, 4, 7, 5, 0)
 COLLECT = 6
 STAGE_AT = (0.0, 3.0, 6.2, 11.7, 17.0, 20.0, 23.2)
-PIECE_GAP = 1.3
+PIECE_GAP = 0.9
 GRAD_LAG = 10.4
 OPPOSITE = (3, 4, 5, 0, 1, 2)
 HANDS = ((-1, 6, 9, 0), (-2, 9, 11, 1), (1, 11, 14, 3), (2, 14, 15, 4))
 VMEM_BYTES = 62 << 20
-CUTS = 2
 Y, Z = 2, 16
 
 norm_eps = 1e-06
@@ -68,19 +67,17 @@
     g_hbm,
     qg_hbm,
     kg_hbm,
-    gq_hbm,
-    gk_hbm,
-    gv_hbm,
-    gain_q_hbm,
-    gain_k_hbm,
+    out_q,
+    out_k,
+    out_v,
+    gain_q_out,
+    gain_k_out,
     q_in,
     k_in,
     v_in,
     g_in,
     qg_ref,
     kg_ref,
-    gain_q_out,
-    gain_k_out,
     feat_q,
     feat_k,
     inv_q,
@@ -89,9 +86,6 @@
     scaled_hi,
     scaled_lo,
     grad_f,
-    out_q,
-    out_k,
-    out_v,
     gain_row,
     gain_col,
     kt_col,
@@ -109,7 +103,6 @@
     three,
     sizes,
     load_sem,
-    store_sem,
     send_sem,
     big_recv,
     small_recv,
@@ -395,7 +388,7 @@
     step(0, 0)
     pl.semaphore_wait(far_sem, 2)
     ar1 = small_stride(1, ar1, one_a, one_b)
-    step(0, 1, 2, 3, 0, 1, 2, 3)
+    step(0, *A[1:], *A)
 
     loads[5].wait()
     key_total = small_done(ar1, one_b)
@@ -471,7 +464,7 @@
         unit = x_in[rows_of(h), :].astype(F32) * inverse
         upstream = jnp.where(feat > 0, grad, 0.0) * gain(h)
         mean = jnp.sum(upstream * unit, axis=0, keepdims=True) * (1.0 / HEAD_DIM)
-        out[rows_of(h), :] = (inverse * (upstream - unit * mean)).astype(BF16)
+        out[0, rows_of(h), :] = (inverse * (upstream - unit * mean)).astype(BF16)
 
     def grad_queries(heads):
         for h in heads:
@@ -490,9 +483,14 @@
     go_on(4)
     ar2 = small_stride(3, ar2, two_a, two_b)
     grad_queries(range(5, HEADS))
-    store_q = pltpu.make_async_copy(out_q, gq_hbm.at[0], store_sem.at[0])
-    store_q.start()
     go_on(5)
+
+    total = small_done(ar2, two_b)
+    three[dp] = total[0:16]
+    ref = three.at[dp, pl.ds(0, HEADS)]
+    ar3 = go(
+        small_recv.at[4], [(ref, ref, (lax.rem(dp + r, dps), space)) for r in range(1, dps)]
+    )
 
     for p in pieces:
         step(1, p)
@@ -500,25 +498,14 @@
             gs_hi, gs_lo = split(take(1, h))
             value = v_in[rows_of(h), :]
             feat = feat_k[rows_of(h), :]
-            out_v[rows_of(h), :] = (dot(gs_hi, feat, TN) + dot(gs_lo, feat, TN)).astype(BF16)
+            out_v[0, rows_of(h), :] = (dot(gs_hi, feat, TN) + dot(gs_lo, feat, TN)).astype(BF16)
             grad_f[rows_of(h), :] = dot(gs_hi, value, NN) + dot(gs_lo, value, NN)
-    store_v = pltpu.make_async_copy(out_v, gv_hbm.at[0], store_sem.at[1])
-    store_v.start()
-
-    total = small_done(ar2, two_b)
-    three[dp] = total[0:16]
-    ref = three.at[dp]
-    ar3 = go(
-        small_recv.at[4], [(ref, ref, (lax.rem(dp + r, dps), space)) for r in range(1, dps)]
-    )
 
     gkt_col = jnp.transpose(total)
     for h in range(HEADS):
         feat = feat_k[rows_of(h), :].astype(F32)
         grad = grad_f[rows_of(h), :] + gkt_col[0:HEAD_DIM, HEADS + h : HEADS + h + 1]
         norm_backward(k_in, inv_k, k_gain, feat, grad, out_k, h)
-    store_k = pltpu.make_async_copy(out_k, gk_hbm.at[0], store_sem.at[2])
-    store_k.start()
 
     land(ar3)
     total = three[0]
@@ -531,32 +518,16 @@
         cut = pl.ds(h * HEAD_DIM, HEAD_DIM)
         gain_q_out[cut] = grad_q_gain[h]
         gain_k_out[cut] = grad_k_gain[h]
-    store_gains = [
-        pltpu.make_async_copy(gain_q_out, gain_q_hbm, store_sem.at[3]),
-        pltpu.make_async_copy(gain_k_out, gain_k_hbm, store_sem.at[4]),
+    wait_rows(send_sem, sent[0])
+
+
+def hand_over(*refs):
+    sources, results, sem = refs[:5], refs[5:10], refs[10]
+    stores = [
+        pltpu.make_async_copy(src, dst, sem.at[i])
+        for i, (src, dst) in enumerate(zip(sources, results))
     ]
-    for store in store_gains:
-        store.start()
-
-    wait_rows(send_sem, sent[0])
-    for store in (store_q, store_v, store_k, *store_gains):
-        store.wait()
-
-
-def hand_over(*refs):
-    sources, results, held, load_sem, store_sem = refs[:3], refs[3:6], *refs[6:]
-    rows = CH // CUTS
-    loads, stores = [], []
-    for i, (src, dst) in enumerate(zip(sources, results)):
-        for part in range(CUTS):
-            cut = pl.ds(part * rows, rows)
-            n = i * CUTS + part
-            loads.append(pltpu.make_async_copy(src.at[0, cut], held.at[i, cut], load_sem.at[n]))
-            stores.append(pltpu.make_async_copy(held.at[i, cut], dst.at[0, cut], store_sem.at[n]))
-    for load in loads:
-        load.start()
-    for load, store in zip(loads, stores):
-        load.wait()
+    for store in stores:
         store.start()
     for store in stores:
         store.wait()
@@ -569,6 +540,9 @@
     all_rows = clip_tokens * dps * queries.shape[0]
     anywhere = pl.BlockSpec(memory_space=pl.ANY)
     big = jax.ShapeDtypeStruct(queries.shape, BF16)
+    big_here = pltpu.VMEM(queries.shape, BF16)
+    row_here = pltpu.VMEM((CH,), F32)
+    here = pl.BlockSpec(memory_space=pltpu.VMEM)
     row = jax.ShapeDtypeStruct((CH,), F32)
     vm = pltpu.VMEM
     dma = pltpu.SemaphoreType.DMA
@@ -576,18 +550,16 @@
     def run(*refs):
         kernel(clip_tokens, all_rows, dps, *refs)
 
-    *grads, gain_q, gain_k = pl.pallas_call(
+    results = pl.pallas_call(
         run,
-        out_shape=(big, big, big, row, row),
+        out_shape=(big_here, big_here, big_here, row_here, row_here),
         in_specs=[anywhere] * 6,
-        out_specs=(anywhere,) * 5,
+        out_specs=(here,) * 5,
         scratch_shapes=[
             vm((CH, tokens), BF16),
             vm((CH, tokens), BF16),
             vm((CH, tokens), BF16),
             vm((CH, tokens), BF16),
-            vm((CH,), F32),
-            vm((CH,), F32),
             vm((CH,), F32),
             vm((CH,), F32),
             vm((CH, tokens), BF16),
@@ -598,9 +570,6 @@
             vm((CH, tokens), BF16),
             vm((CH, tokens), BF16),
             vm((CH, tokens), F32),
-            vm((CH, tokens), BF16),
-            vm((CH, tokens), BF16),
-            vm((CH, tokens), BF16),
             vm((32, LANES), F32),
             vm((LANES, 32), F32),
             vm((LANES, 16), F32),
@@ -618,7 +587,6 @@
             vm((dps, 16, LANES), F32),
             vm((2 * 2048 + 640, LANES), F32),
             dma((6,)),
-            dma((5,)),
             dma(()),
             dma((2, PIECES, STAGES)),
             dma((5,)),
@@ -629,16 +597,15 @@
         ),
         name="linear_attention_backward",
     )(queries, keys, values, out_grad, q_gain, k_gain)
-    grads = pl.pallas_call(
+    return pl.pallas_call(
         hand_over,
-        out_shape=(big, big, big),
-        in_specs=[anywhere] * 3,
-        out_specs=(anywhere,) * 3,
-        scratch_shapes=[vm((3, CH, tokens), BF16), dma((3 * CUTS,)), dma((3 * CUTS,))],
-        compiler_params=pltpu.CompilerParams(vmem_limit_bytes=VMEM_BYTES),
+        out_shape=(big, big, big, row, row),
+        in_specs=[here] * 5,
+        out_specs=(anywhere,) * 5,
+        scratch_shapes=[dma((5,))],
+        compiler_params=pltpu.CompilerParams(vmem_limit_bytes=4 << 20),
         name="hand_over",
-    )(*grads)
-    return (*grads, gain_q, gain_k)
+    )(*results)
 
 
 def solution(mesh):

time: 74 us -> 69.5 us (0.939)
  Pallas kernels: 71.8 us -> 68.7 us
  local copies, waits for them, and re-layouts: 1.29 us -> 0 us
    pallas_call x2, Pallas kernels: 71.8 us -> 68.7 us  [the longest x1 67.5 us: local(): pl.pallas_call(run, out_shape=(big_here, big_here, big_here, row_here, ro...]
    unnamed x6 -> x0, local copies, waits for them, and re-layouts: 1.29 us -> none
where the time goes in v4:
time: 69.5 us; the launch traced here: 69.3 us
  Pallas kernels  68.7 us (99%)
    pallas_call x1, Pallas kernels, local(): pl.pallas_call(run, out_shape=(big_here, big_here, big_here, row_here, ro...  67.5 us

profile of v4, /device:TPU:1, one launch (start us, length us, event | category | flops | bytes accessed | tf_op | source)
XLA Modules:
  0.0 69.3 jit_solution(1031502482796765)
XLA Ops:
  0.6 67.5 %linear_attention_backward.1 = (bf16[1,1120,256]{2,1,0:T(8,128)(2,1)S(1)}, bf16[1,1120,256]{2,1,0:T(8,128)(2,1)S(1)}, bf16[1,1120,256]{2,1,0:T(8,128)(2,1)S(1)}, f32[1120]{0:T(1024)S(1)}, f32[1120]{0:T(1024)S(1)}) custom-call(bf16[1,1120,256]{2,1,0:T(8,128)(2,1)} %refs_0_.1, bf16[1,1120,256]{2,1,0:T(8,128)(2,1)} %refs_1_.1, bf16[1,1120,256]{2,1,0:T(8,128)(2,1)} %refs_2_.1, ...), custom_call_target="tpu_custom_call" | custom-call | tf_op jit(solution)/shard_map/linear_attention_backward/pallas_call | solution.py:553
  68.1 1.2 %hand_over.1 = (bf16[1,1120,256]{2,1,0:T(8,128)(2,1)}, bf16[1,1120,256]{2,1,0:T(8,128)(2,1)}, bf16[1,1120,256]{2,1,0:T(8,128)(2,1)}, f32[1120]{0:T(1024)}, f32[1120]{0:T(1024)}) custom-call(bf16[1,1120,256]{2,1,0:T(8,128)(2,1)S(1)} %get-tuple-element.10.refs_0_, bf16[1,1120,256]{2,1,0:T(8,128)(2,1)S(1)} %get-tuple-element.11.refs_1_, ...), custom_call_target="tpu_custom_call" | custom-call | tf_op jit(solution)/shard_map/hand_over/pallas_call | solution.py:600

commit v5 on v4

--- a/solution.py
+++ b/solution.py
@@ -15,7 +15,7 @@
 SPARE = LANES - HEAD_DIM
 HOSTS = HEAD_DIM // SPARE
 ROWS = 1024
-PIECES = 4
+PIECES = 8
 PIECE = ROWS // PIECES
 HALF = PIECE // 2
 OWN = HALF // 16
@@ -23,7 +23,7 @@
 SPOTS = (-1, -3, -6, 1, 3, 6, -2, -4, -7, -5, -8, 2, 4, 7, 5, 0)
 COLLECT = 6
 STAGE_AT = (0.0, 3.0, 6.2, 11.7, 17.0, 20.0, 23.2)
-PIECE_GAP = 0.9
+PIECE_GAP = 0.45
 GRAD_LAG = 10.4
 OPPOSITE = (3, 4, 5, 0, 1, 2)
 HANDS = ((-1, 6, 9, 0), (-2, 9, 11, 1), (1, 11, 14, 3), (2, 14, 15, 4))

time: 69.5 us -> 68.5 us (0.986)
  Pallas kernels: 68.7 us -> 67.7 us
    pallas_call x1, Pallas kernels: 67.5 us -> 66.5 us  [local(): pl.pallas_call(run, out_shape=(big_here, big_here, big_here, row_here, ro...]
where the time goes in v5:
time: 68.5 us; the launch traced here: 68.4 us
  Pallas kernels  67.7 us (99%)
    pallas_call x1, Pallas kernels, local(): pl.pallas_call(run, out_shape=(big_here, big_here, big_here, row_here, ro...  66.5 us

profile of v5, /device:TPU:1, one launch (start us, length us, event | category | flops | bytes accessed | tf_op | source)
XLA Modules:
  0.0 68.4 jit_solution(7684464317069527353)
XLA Ops:
  0.6 66.5 %linear_attention_backward.1 = (bf16[1,1120,256]{2,1,0:T(8,128)(2,1)S(1)}, bf16[1,1120,256]{2,1,0:T(8,128)(2,1)S(1)}, bf16[1,1120,256]{2,1,0:T(8,128)(2,1)S(1)}, f32[1120]{0:T(1024)S(1)}, f32[1120]{0:T(1024)S(1)}) custom-call(bf16[1,1120,256]{2,1,0:T(8,128)(2,1)} %refs_0_.1, bf16[1,1120,256]{2,1,0:T(8,128)(2,1)} %refs_1_.1, bf16[1,1120,256]{2,1,0:T(8,128)(2,1)} %refs_2_.1, ...), custom_call_target="tpu_custom_call" | custom-call | tf_op jit(solution)/shard_map/linear_attention_backward/pallas_call | solution.py:553
  67.1 1.2 %hand_over.1 = (bf16[1,1120,256]{2,1,0:T(8,128)(2,1)}, bf16[1,1120,256]{2,1,0:T(8,128)(2,1)}, bf16[1,1120,256]{2,1,0:T(8,128)(2,1)}, f32[1120]{0:T(1024)}, f32[1120]{0:T(1024)}) custom-call(bf16[1,1120,256]{2,1,0:T(8,128)(2,1)S(1)} %get-tuple-element.10.refs_0_, bf16[1,1120,256]{2,1,0:T(8,128)(2,1)S(1)} %get-tuple-element.11.refs_1_, ...), custom_call_target="tpu_custom_call" | custom-call | tf_op jit(solution)/shard_map/hand_over/pallas_call | solution.py:600
